TPU v7x, 32 devices: a whole 2x2x4 slice. The times are simulated.
32 devices in a mesh: dp: 16 (over z, y, x), mp: 2 (over core).
Axes of the slice: x: 2, y: 2, z: 4, core: 2. Of those that a mesh axis runs over, the one named last changes fastest.
Arguments:
- sentence_layer_entry: bfloat16 [8192, 768], P('dp'), may hold values from -6 to 6
- sentence_word_ids: int32 [8192], P('dp'), may hold values from 0 to 31999, as said below
- picture_tile_activations: bfloat16 [512, 145, 768], P(('dp', 'mp')), may hold values from -6 to 6
- picture_detail_flag: int32 [512], P(('dp', 'mp')), may hold values 0 or 1
- matched_picture_ids: int32 [512], P('dp'), may hold values from 0 to 511, each once
- mixer_layernorm_gamma: float32 [768], replicated, may hold values from 0.5 to 1.5
- mixer_layernorm_offset: float32 [768], replicated, may hold values from -1.5 to 1.5
- mixer_triple_matrix: bfloat16 [3, 768, 768], P(None, None, 'mp'), may hold values from -0.21875 to 0.21875
- mixer_pair_offsets: float32 [2, 768], P(None, 'mp'), may hold values from -1.5 to 1.5
- mixer_result_matrix: bfloat16 [768, 768], P('mp'), may hold values from -0.4375 to 0.4375
- mixer_result_offset: float32 [768], replicated, may hold values from -1.5 to 1.5
- perceptron_layernorm_gamma: float32 [768], replicated, may hold values from 0.5 to 1.5
- perceptron_layernorm_offset: float32 [768], replicated, may hold values from -1.5 to 1.5
- widening_matrix: bfloat16 [768, 3072], P(None, 'mp'), may hold values from -0.21875 to 0.21875
- widening_offset: float32 [3072], P('mp'), may hold values from -1.5 to 1.5
- narrowing_matrix: bfloat16 [3072, 768], P('mp'), may hold values from -0.109375 to 0.109375
- narrowing_offset: float32 [768], replicated, may hold values from -1.5 to 1.5
- sharpening_log: float32 [1], replicated, may hold values from 3.7 to 4.2
- locked_layernorm_gammas: float32 [2, 768], replicated, may hold values from 0.5 to 1.5
- locked_mixer_triple_matrix: bfloat16 [3, 768, 768], replicated, may hold values from -0.21875 to 0.21875
- locked_mixer_result_matrix: bfloat16 [768, 768], replicated, may hold values from -0.875 to 0.875
- locked_widening_matrix: bfloat16 [768, 3072], replicated, may hold values from -0.21875 to 0.21875
- locked_narrowing_matrix: bfloat16 [3072, 768], replicated, may hold values from -0.109375 to 0.109375
Outputs:
- training_error: float32 [1], replicated
- grad_input: float32 [8192, 768], P('dp')
- grad_qkv: float32 [3, 768, 768], P(None, None, 'mp')
- grad_b_qv: float32 [2, 768], P(None, 'mp')
- grad_w_out: float32 [768, 768], P('mp')
- grad_b_out: float32 [768], replicated
- grad_w_up: float32 [768, 3072], P(None, 'mp')
- grad_b_up: float32 [3072], P('mp')
- grad_w_down: float32 [3072, 768], P('mp')
- grad_b_down: float32 [768], replicated
- grad_ln1_gain: float32 [768], replicated
- grad_ln1_bias: float32 [768], replicated
- grad_ln2_gain: float32 [768], replicated
- grad_ln2_bias: float32 [768], replicated
- grad_temperature: float32 [1], replicated
Inputs may be any that keep to these rules, and one draw needn't show every extreme that they name: `sentence_word_ids`: in each caption of 16 positions the nonzero ids form a prefix of 2 or more positions and 0 fills the rest; in every draw some caption has no 0 and some caption has exactly 2 nonzero ids.
All inputs are finite; a program needn't handle non-finite values. No bound on the sum of `picture_detail_flag` on one device may be relied on, other than what follows from the above.
Results may differ from a plain program's by a relative error of at most 0.0095.
The roundings to bfloat16 on the way count: a program that leaves them out, or rounds other values in their place, can miss the bound.
Values may be sent and summed in bfloat16 or wider, within the bound.
No kernel may reach another device: no remote copies, remote signals or barrier semaphores. Data moves between devices by JAX's collectives and lax.ppermute only.
A program may use at most 128 MiB of HBM per device.

v0:
```python
import jax
import jax.numpy as jnp
from jax import lax
from jax.sharding import PartitionSpec as P

HEAD = 64
IMG_TOK = 145
LOW_TOK = 50


EPS_TEXT = 1e-05
EPS_UNIT = 1e-06
MASKED_SCORE = -1e30


def layer_norm(values, gain, shift, epsilon):
    centered = values - jnp.mean(values, axis=-1, keepdims=True)
    variance = jnp.mean(centered * centered, axis=-1, keepdims=True)
    return centered * lax.rsqrt(variance + epsilon) * gain + shift


def text_norm(values, gain, shift):
    return layer_norm(values, gain, shift, EPS_TEXT)


def gelu_exact(values):
    return jax.nn.gelu(values, approximate=False)


def image_block(
    tokens,
    live_len,
    locked_layernorm_gammas,
    locked_mixer_triple_matrix,
    locked_mixer_result_matrix,
    locked_widening_matrix,
    locked_narrowing_matrix,
):
    batch_size, seq_len, model_width = tokens.shape
    heads_all = model_width // HEAD
    tokens_f = tokens.astype(jnp.float32)
    normed = layer_norm(tokens_f, locked_layernorm_gammas[0], 0.0, EPS_UNIT).astype(jnp.bfloat16)

    def project(weight):
        return (
            jnp.einsum("bsd,de->bse", normed, weight, preferred_element_type=jnp.float32)
            .astype(jnp.bfloat16)
            .reshape(batch_size, seq_len, heads_all, HEAD)
        )

    queries, keys_in, values = (
        project(locked_mixer_triple_matrix[0]),
        project(locked_mixer_triple_matrix[1]),
        project(locked_mixer_triple_matrix[2]),
    )
    scores = jnp.einsum(
        "bqhe,bkhe->bhqk", queries, keys_in, preferred_element_type=jnp.float32
    ) * HEAD ** (-0.5)
    key_live = jnp.arange(seq_len, dtype=jnp.int32)[None, :] < live_len[:, None]
    scores = jnp.where(key_live[:, None, None, :], scores, MASKED_SCORE)
    soft_weights = jax.nn.softmax(scores, axis=-1).astype(jnp.bfloat16)
    mixed_heads = (
        jnp.einsum("bhqk,bkhe->bqhe", soft_weights, values, preferred_element_type=jnp.float32)
        .astype(jnp.bfloat16)
        .reshape(batch_size, seq_len, model_width)
    )
    residual = tokens_f + jnp.einsum(
        "bsc,cd->bsd", mixed_heads, locked_mixer_result_matrix, preferred_element_type=jnp.float32
    )
    normed2 = layer_norm(residual, locked_layernorm_gammas[1], 0.0, EPS_UNIT).astype(jnp.bfloat16)
    hidden = gelu_exact(
        jnp.einsum(
            "bsd,df->bsf", normed2, locked_widening_matrix, preferred_element_type=jnp.float32
        )
    ).astype(jnp.bfloat16)
    output = residual + jnp.einsum(
        "bsf,fd->bsd", hidden, locked_narrowing_matrix, preferred_element_type=jnp.float32
    )
    pool_weight = key_live.astype(jnp.float32) / live_len.astype(jnp.float32)[:, None]
    pooled = jnp.sum(output * pool_weight[:, :, None], axis=1)
    return (pooled * lax.rsqrt(jnp.sum(pooled * pooled, axis=-1, keepdims=True) + EPS_UNIT)).astype(
        jnp.bfloat16
    )


def online_update(old_max, pairwise_score_matrix):
    new_max = jnp.maximum(old_max, jnp.max(pairwise_score_matrix, axis=1))
    new_sum = jnp.sum(jnp.exp(pairwise_score_matrix - new_max[:, None]), axis=1)
    return (new_max, new_sum)


def local(
    sentence_layer_entry,
    sentence_word_ids,
    picture_tile_activations,
    picture_detail_flag,
    matched_picture_ids,
    mixer_layernorm_gamma,
    mixer_layernorm_offset,
    mixer_triple_matrix,
    mixer_pair_offsets,
    mixer_result_matrix,
    mixer_result_offset,
    perceptron_layernorm_gamma,
    perceptron_layernorm_offset,
    widening_matrix,
    widening_offset,
    narrowing_matrix,
    narrowing_offset,
    sharpening_log,
    locked_layernorm_gammas,
    locked_mixer_triple_matrix,
    locked_mixer_result_matrix,
    locked_widening_matrix,
    locked_narrowing_matrix,
):
    captions = matched_picture_ids.shape[0]
    sentence_feature_matrix = sentence_layer_entry.shape[0]
    cap_len = sentence_feature_matrix // captions
    model_width = sentence_layer_entry.shape[1]
    local_heads = mixer_triple_matrix.shape[2] // HEAD
    local_width = local_heads * HEAD
    head_scale = HEAD ** (-0.5)
    all_pairs = captions * lax.axis_size("dp")
    valid = (sentence_word_ids != 0).reshape(captions, cap_len)
    valid_f = valid.astype(jnp.float32)
    pool_weight = valid_f / jnp.sum(valid_f, axis=1, keepdims=True)
    local_images = picture_tile_activations.shape[0]
    img_block = 4
    image_live = jnp.where(picture_detail_flag == 1, IMG_TOK, LOW_TOK).astype(jnp.int32)

    def image_group(pieces):
        return image_block(
            pieces[0],
            pieces[1],
            locked_layernorm_gammas,
            locked_mixer_triple_matrix,
            locked_mixer_result_matrix,
            locked_widening_matrix,
            locked_narrowing_matrix,
        )

    image_half = lax.map(
        image_group,
        (
            picture_tile_activations.reshape(
                local_images // img_block, img_block, picture_tile_activations.shape[1], model_width
            ),
            image_live.reshape(local_images // img_block, img_block),
        ),
    ).reshape(local_images, model_width)
    picture_feature_matrix = lax.all_gather(image_half, "mp", axis=0, tiled=True)

    def to_heads(values):
        return values.reshape(captions, cap_len, local_heads, HEAD)

    x_float = sentence_layer_entry.astype(jnp.float32)
    normed_f, norm1_pull = jax.vjp(
        text_norm, x_float, mixer_layernorm_gamma, mixer_layernorm_offset
    )
    normed = normed_f.astype(jnp.bfloat16)
    queries = to_heads(
        (
            jnp.dot(normed, mixer_triple_matrix[0], preferred_element_type=jnp.float32)
            + mixer_pair_offsets[0]
        ).astype(jnp.bfloat16)
    )
    keys_low = to_heads(
        jnp.dot(normed, mixer_triple_matrix[1], preferred_element_type=jnp.float32).astype(
            jnp.bfloat16
        )
    )
    values_low = to_heads(
        (
            jnp.dot(normed, mixer_triple_matrix[2], preferred_element_type=jnp.float32)
            + mixer_pair_offsets[1]
        ).astype(jnp.bfloat16)
    )
    scores = (
        jnp.einsum("gqhe,gkhe->ghqk", queries, keys_low, preferred_element_type=jnp.float32)
        * head_scale
    )
    scores = jnp.where(valid[:, None, None, :], scores, MASKED_SCORE)
    soft_f = jax.nn.softmax(scores, axis=-1)
    soft_low = soft_f.astype(jnp.bfloat16)
    mixed_heads = jnp.einsum(
        "ghqk,gkhe->gqhe", soft_low, values_low, preferred_element_type=jnp.float32
    ).astype(jnp.bfloat16)
    mixed_rows = mixed_heads.reshape(sentence_feature_matrix, local_width)
    attended = lax.psum(
        jnp.dot(mixed_rows, mixer_result_matrix, preferred_element_type=jnp.float32), "mp"
    )
    residual = x_float + attended + mixer_result_offset
    normed2_f, norm2_pull = jax.vjp(
        text_norm, residual, perceptron_layernorm_gamma, perceptron_layernorm_offset
    )
    normed2 = normed2_f.astype(jnp.bfloat16)
    pre_act = (
        jnp.dot(normed2, widening_matrix, preferred_element_type=jnp.float32) + widening_offset
    )
    hidden_f, gelu_pull = jax.vjp(gelu_exact, pre_act)
    hidden = hidden_f.astype(jnp.bfloat16)
    branch_two = lax.psum(
        jnp.dot(hidden, narrowing_matrix, preferred_element_type=jnp.float32), "mp"
    )
    output = residual + branch_two + narrowing_offset

    def pool_unit(rows):
        pooled = jnp.sum(
            rows.reshape(captions, cap_len, model_width) * pool_weight[:, :, None], axis=1
        )
        return pooled * lax.rsqrt(jnp.sum(pooled * pooled, axis=-1, keepdims=True) + EPS_UNIT)

    sentence_normalized_matrix, pool_pull = jax.vjp(pool_unit, output)
    text_emb = sentence_normalized_matrix.astype(jnp.bfloat16)
    sharpening_multiplier = jnp.exp(sharpening_log[0])
    empty_stats = jnp.full((captions,), MASKED_SCORE, jnp.float32)
    row_max = empty_stats
    col_max = empty_stats
    text_piece = lax.all_gather(text_emb, "dp", axis=0, tiled=True)
    image_piece = lax.all_gather(picture_feature_matrix, "dp", axis=0, tiled=True)
    piece_rows = image_piece.shape[0]
    per_sentence_scores = sharpening_multiplier * jnp.einsum(
        "cd,nd->cn", text_emb, image_piece, preferred_element_type=jnp.float32
    )
    row_max, row_sum = online_update(row_max, per_sentence_scores)
    is_positive = matched_picture_ids[:, None] == jnp.arange(piece_rows, dtype=jnp.int32)[None, :]
    positive = jnp.sum(jnp.where(is_positive, per_sentence_scores, 0.0))
    per_picture_scores = sharpening_multiplier * jnp.einsum(
        "cd,nd->cn", picture_feature_matrix, text_piece, preferred_element_type=jnp.float32
    )
    col_max, col_sum = online_update(col_max, per_picture_scores)
    row_max, row_sum, col_max, col_sum, positive = (row_max, row_sum, col_max, col_sum, positive)
    row_lse = row_max + jnp.log(row_sum)
    col_lse = col_max + jnp.log(col_sum)
    local_loss = (jnp.sum(row_lse) + jnp.sum(col_lse) - 2.0 * positive).reshape(1)
    image_piece = lax.all_gather(
        picture_feature_matrix.astype(jnp.float32), "dp", axis=0, tiled=True
    )
    col_piece = lax.all_gather(col_lse, "dp", axis=0, tiled=True)
    piece_rows = image_piece.shape[0]
    image_low = image_piece.astype(jnp.bfloat16)
    pairwise_score_matrix = sharpening_multiplier * jnp.einsum(
        "cd,nd->cn", text_emb, image_low, preferred_element_type=jnp.float32
    )
    is_positive = (
        matched_picture_ids[:, None] == jnp.arange(piece_rows, dtype=jnp.int32)[None, :]
    ).astype(jnp.float32)
    score_derivative = (
        jnp.exp(pairwise_score_matrix - row_lse[:, None])
        + jnp.exp(pairwise_score_matrix - col_piece[None, :])
        - 2.0 * is_positive
    ) / (2.0 * all_pairs)
    agreement_derivative = (score_derivative * sharpening_multiplier).astype(jnp.bfloat16)
    text_grad = jnp.dot(agreement_derivative, image_low, preferred_element_type=jnp.float32)
    temp_grad = jnp.sum(score_derivative * pairwise_score_matrix)
    text_grad, temp_grad = (text_grad, temp_grad)
    (grad_output,) = pool_pull(text_grad)
    grad_branch2 = grad_output.astype(jnp.bfloat16)
    grad_b_down = jnp.sum(grad_branch2.astype(jnp.float32), axis=0)
    grad_w_down = jnp.einsum("tf,td->fd", hidden, grad_branch2, preferred_element_type=jnp.float32)
    (grad_pre,) = gelu_pull(
        jnp.einsum("td,fd->tf", grad_branch2, narrowing_matrix, preferred_element_type=jnp.float32)
    )
    grad_pre_low = grad_pre.astype(jnp.bfloat16)
    grad_b_up = jnp.sum(grad_pre_low.astype(jnp.float32), axis=0)
    grad_w_up = jnp.einsum("td,tf->df", normed2, grad_pre_low, preferred_element_type=jnp.float32)
    grad_normed2 = lax.psum(
        jnp.einsum("tf,df->td", grad_pre_low, widening_matrix, preferred_element_type=jnp.float32),
        "mp",
    )
    grad_res_norm, grad_ln2_gain, grad_ln2_bias = norm2_pull(grad_normed2)
    grad_residual = grad_output + grad_res_norm
    grad_branch1 = grad_residual.astype(jnp.bfloat16)
    grad_b_out = jnp.sum(grad_branch1.astype(jnp.float32), axis=0)
    grad_w_out = jnp.einsum(
        "tc,td->cd", mixed_rows, grad_branch1, preferred_element_type=jnp.float32
    )
    grad_mixed = to_heads(
        jnp.einsum(
            "td,cd->tc", grad_branch1, mixer_result_matrix, preferred_element_type=jnp.float32
        ).astype(jnp.bfloat16)
    )
    grad_soft = jnp.einsum(
        "gqhe,gkhe->ghqk", grad_mixed, values_low, preferred_element_type=jnp.float32
    )
    grad_values = jnp.einsum(
        "ghqk,gqhe->gkhe", soft_low, grad_mixed, preferred_element_type=jnp.float32
    ).astype(jnp.bfloat16)
    grad_scores = (
        soft_f * (grad_soft - jnp.sum(grad_soft * soft_f, axis=-1, keepdims=True))
    ).astype(jnp.bfloat16)
    grad_queries = (
        jnp.einsum("ghqk,gkhe->gqhe", grad_scores, keys_low, preferred_element_type=jnp.float32)
        * head_scale
    ).astype(jnp.bfloat16)
    grad_keys = (
        jnp.einsum("ghqk,gqhe->gkhe", grad_scores, queries, preferred_element_type=jnp.float32)
        * head_scale
    ).astype(jnp.bfloat16)
    flat_grads = (
        grad_queries.reshape(sentence_feature_matrix, local_width),
        grad_keys.reshape(sentence_feature_matrix, local_width),
        grad_values.reshape(sentence_feature_matrix, local_width),
    )
    grad_qkv = jnp.stack(
        [
            jnp.einsum("td,tc->dc", normed, part_grad, preferred_element_type=jnp.float32)
            for part_grad in flat_grads
        ]
    )
    grad_b_qv = jnp.stack(
        [
            jnp.sum(flat_grads[0].astype(jnp.float32), axis=0),
            jnp.sum(flat_grads[2].astype(jnp.float32), axis=0),
        ]
    )
    normed_terms = jnp.einsum(
        "tc,dc->td", flat_grads[0], mixer_triple_matrix[0], preferred_element_type=jnp.float32
    )
    normed_terms = normed_terms + jnp.einsum(
        "tc,dc->td", flat_grads[1], mixer_triple_matrix[1], preferred_element_type=jnp.float32
    )
    normed_terms = normed_terms + jnp.einsum(
        "tc,dc->td", flat_grads[2], mixer_triple_matrix[2], preferred_element_type=jnp.float32
    )
    grad_normed = lax.psum(normed_terms, "mp")
    grad_in_norm, grad_ln1_gain, grad_ln1_bias = norm1_pull(grad_normed)
    grad_input = grad_residual + grad_in_norm
    summed = lax.psum(
        (
            grad_qkv,
            grad_b_qv,
            grad_w_out,
            grad_b_out,
            grad_w_up,
            grad_b_up,
            grad_w_down,
            grad_b_down,
            grad_ln1_gain,
            grad_ln1_bias,
            grad_ln2_gain,
            grad_ln2_bias,
            temp_grad.reshape(1),
            local_loss,
        ),
        "dp",
    )
    training_error = summed[13] / (2.0 * all_pairs)
    return (
        training_error,
        grad_input,
        summed[0],
        summed[1],
        summed[2],
        summed[3],
        summed[4],
        summed[5],
        summed[6],
        summed[7],
        summed[8],
        summed[9],
        summed[10],
        summed[11],
        summed[12],
    )


def solution(mesh):
    placed = (
        P("dp", None),
        P("dp"),
        P(("dp", "mp"), None, None),
        P(("dp", "mp")),
        P("dp"),
        P(),
        P(),
        P(None, None, "mp"),
        P(None, "mp"),
        P("mp", None),
        P(),
        P(),
        P(),
        P(None, "mp"),
        P("mp"),
        P("mp", None),
        P(),
        P(),
        P(),
        P(),
        P(),
        P(),
        P(),
    )
    return jax.shard_map(
        local,
        mesh=mesh,
        in_specs=placed,
        out_specs=(
            P(),
            P("dp", None),
            P(None, None, "mp"),
            P(None, "mp"),
            P("mp", None),
            P(),
            P(None, "mp"),
            P("mp"),
            P("mp", None),
            P(),
            P(),
            P(),
            P(),
            P(),
            P(),
        ),
        check_vma=False,
    )
```

profile of v0, /device:TPU:0, one launch (start us, length us, event | category | flops | bytes accessed | tf_op | source)
XLA Modules:
  0.0 1013.4 jit_solution(11142870103945696064)
XLA Ops:
  42.2 17.5 %all-reduce.9.cloned.1.call-done = f32[512,768]{1,0:T(8,128)} async-done(((f32[512,768]{1,0:T(8,128)}), f32[512,768]{1,0:T(8,128)}) %all-reduce.9.cloned.1.call-update) | async-done | bytes 1572880 | tf_op jit(solution)/shard_map/psum | solution.py:190
  62.6 9.4 multiply_convert_fusion.2
  75.9 252.9 %while.10 = (s32[]{:T(128)}, bf16[4,4,768]{2,1,0:T(4,128)(2,1)S(1)}, bf16[4,4,145,768]{3,2,1,0:T(8,128)(2,1)}, f32[2,768]{1,0:T(2,128)S(1)}, bf16[3,768,768]{2,1...) while((s32[]{:T(128)}, ...), condition=%wide.region_20.21_spmd, body=%wide.region_11.20_spmd.sunk | while | flops 8638695424 | bytes 96550040 | solution.py:143
  113.8 7.9 fusion.262
  129.4 5.1 fusion.265
  134.5 19.4 %multiply_reduce_fusion.15 = f32[4,768]{1,0:T(4,128)S(1)} fusion(f32[4,145,768]{2,1,0:T(8,128)S(1)} %get-tuple-element.218, bf16[3072,768]{1,0:T(8,128)(2,1)S(1)} %bitcast.188, f32[4,145,3072]{2,1,0:T(8,128)S(1)} %get-tuple-element.221, u8[145,3072]{1,0:T(8,128)(4,1)S(1)} %get-tuple-element.222, u8[145,3072]{1,0:T(8,128)(4,1)S(1)} %get-tuple-element.223, ...), kind=kOutput, calls=%fused_computation.46.clone.1 | convolution fusion | flops 2862839808 | bytes 14532880 | tf_op jit(solution)/shard_map/while/body/eval_jaxpr/bsf,fd->bsd/dot_general | solution.py:76
  170.0 7.9 fusion.262
  185.6 5.1 fusion.265
  190.7 19.4 %multiply_reduce_fusion.15 = f32[4,768]{1,0:T(4,128)S(1)} fusion(f32[4,145,768]{2,1,0:T(8,128)S(1)} %get-tuple-element.218, bf16[3072,768]{1,0:T(8,128)(2,1)S(1)} %bitcast.188, f32[4,145,3072]{2,1,0:T(8,128)S(1)} %get-tuple-element.221, u8[145,3072]{1,0:T(8,128)(4,1)S(1)} %get-tuple-element.222, u8[145,3072]{1,0:T(8,128)(4,1)S(1)} %get-tuple-element.223, ...), kind=kOutput, calls=%fused_computation.46.clone.1 | convolution fusion | flops 2862839808 | bytes 14532880 | tf_op jit(solution)/shard_map/while/body/eval_jaxpr/bsf,fd->bsd/dot_general | solution.py:76
  226.1 7.9 fusion.262
  246.8 19.4 %multiply_reduce_fusion.15 = f32[4,768]{1,0:T(4,128)S(1)} fusion(f32[4,145,768]{2,1,0:T(8,128)S(1)} %get-tuple-element.218, bf16[3072,768]{1,0:T(8,128)(2,1)S(1)} %bitcast.188, f32[4,145,3072]{2,1,0:T(8,128)S(1)} %get-tuple-element.221, u8[145,3072]{1,0:T(8,128)(4,1)S(1)} %get-tuple-element.222, u8[145,3072]{1,0:T(8,128)(4,1)S(1)} %get-tuple-element.223, ...), kind=kOutput, calls=%fused_computation.46.clone.1 | convolution fusion | flops 2862839808 | bytes 14532880 | tf_op jit(solution)/shard_map/while/body/eval_jaxpr/bsf,fd->bsd/dot_general | solution.py:76
  282.3 7.9 fusion.262
  303.0 19.4 %multiply_reduce_fusion.15 = f32[4,768]{1,0:T(4,128)S(1)} fusion(f32[4,145,768]{2,1,0:T(8,128)S(1)} %get-tuple-element.218, bf16[3072,768]{1,0:T(8,128)(2,1)S(1)} %bitcast.188, f32[4,145,3072]{2,1,0:T(8,128)S(1)} %get-tuple-element.221, u8[145,3072]{1,0:T(8,128)(4,1)S(1)} %get-tuple-element.222, u8[145,3072]{1,0:T(8,128)(4,1)S(1)} %get-tuple-element.223, ...), kind=kOutput, calls=%fused_computation.46.clone.1 | convolution fusion | flops 2862839808 | bytes 14532880 | tf_op jit(solution)/shard_map/while/body/eval_jaxpr/bsf,fd->bsd/dot_general | solution.py:76
  333.0 45.8 %all_gather.18 = bf16[512,768]{1,0:T(8,128)(2,1)S(1)} all-gather(bf16[32,768]{1,0:T(8,128)(2,1)S(1)} %all_gather.15), channel_id=1, replica_groups=mesh['dp'=16,'mp'=2] {'dp'}, dimensions={0}, use_global_device_ids=true | all-gather | bytes 835584 | tf_op jit(solution)/shard_map/all_gather | solution.py:237
  378.8 42.6 %all_gather.16 = bf16[512,768]{1,0:T(8,128)(2,1)} all-gather(bf16[32,768]{1,0:T(8,128)(2,1)S(1)} %all_gather.15), channel_id=1, replica_groups=mesh['dp'=16,'mp'=2] {'dp'}, dimensions={0}, use_global_device_ids=true | all-gather | bytes 835584 | tf_op jit(solution)/shard_map/all_gather | solution.py:221
  424.1 42.8 %all_gather.17 = bf16[512,768]{1,0:T(8,128)(2,1)S(1)} all-gather(bf16[32,768]{1,0:T(8,128)(2,1)S(1)} %multiply_convert_fusion.7), channel_id=1, replica_groups=mesh['dp'=16,'mp'=2] {'dp'}, dimensions={0}, use_global_device_ids=true | all-gather | bytes 835584 | tf_op jit(solution)/shard_map/all_gather | solution.py:220
  470.0 36.5 %all-reduce = f32[512]{0:T(512)S(1)} all-reduce(f32[512]{0:T(512)S(1)} %get-tuple-element.129), channel_id=1, replica_groups=mesh['dp'=16,'mp'=2] {'dp'}, use_global_device_ids=true, to_apply=%add | all-reduce | flops 512 | bytes 4096
  508.3 5.4 convert_reduce_fusion.1
  517.6 5.7 fusion.162
  523.2 12.6 %all-reduce.13.cloned.1.call-done = f32[512,768]{1,0:T(8,128)} async-done(((f32[512,768]{1,0:T(8,128)}), f32[512,768]{1,0:T(8,128)}) %all-reduce.13.cloned.1.call-update) | async-done | bytes 1572880 | tf_op jit(solution)/shard_map/psum | solution.py:268
  566.3 5.3 fusion.191
  580.3 7.3 all-reduce.15.cloned.1.call-done
  590.5 83.0 %all-reduce.1 = (f32[1]{0:T(128)}, f32[2,384]{1,0:T(2,128)}, f32[768]{0:T(1024)}, f32[1536]{0:T(1024)}, f32[768]{0:T(1024)}, /*index=5*/f32[768]{0:T(1024)}, f32...) all-reduce(f32[1]{0:T(128)} %bitcast.25, ...), channel_id=1, replica_groups=mesh['dp'=16,'mp'=2] {'dp'}, use_global_device_ids=true, to_apply=%region_28.29 | all-reduce | flops 6914 | bytes 55312 | tf_op jit(solution)/shard_map/psum | solution.py:330
  677.7 317.0 %all-reduce.17.cloned.1.call-done = (f32[3,768,384]{2,1,0:T(8,128)}, f32[384,768]{1,0:T(8,128)}, f32[768,1536]{1,0:T(8,128)}, f32[1536,768]{1,0:T(8,128)}) async-done(((f32[3,768,384]{2,1,0:T(8,128)}, f32[384,768]{1,0:T(8,128)}, f32[768,1536]{1,0:T(8,128)}, f32[1536,768]{1,0:T(8,128)}), (f32[3,768,384]{2,1,0:T(8,128)}, f32[384,768]{1,0:T(8,128)}, f32[768,1536]{1,0:T(8,128)}, ...) | async-done | bytes 14155792 | tf_op jit(solution)/shard_map/psum | solution.py:330
  (379 shorter events, 214.2 us)
Async XLA Ops:
  7.2 55.3 %copy-start = (bf16[768,1536]{1,0:T(8,128)(2,1)S(1)}, bf16[768,1536]{1,0:T(8,128)(2,1)}, u32[]{:S(2)}) copy-start(bf16[768,1536]{1,0:T(8,128)(2,1)} %param.38) | copy-start | bytes 7077892
  7.2 52.5 %all-reduce.9.cloned.1.call-start = ((), (), s32[]{:S(2)}) async-start(), calls=%async_computation | async-start | bytes 3145728 | tf_op jit(solution)/shard_map/psum | solution.py:190
  9.4 7.3 copy-start.33
  11.6 12.9 %copy-start.35 = (pred[32,16]{1,0:T(8,128)(4,1)}, pred[32,16]{1,0:T(8,128)(4,1)S(1)}, u32[]{:S(2)}) copy-start(pred[32,16]{1,0:T(8,128)(4,1)S(1)} %broadcast_in_dim.70) | copy-start | bytes 1540
  36.5 384.9 %all-reduce.11.cloned.1.call-start = ((), (), s32[]{:S(2)}) async-start(), calls=%async_computation.1 | async-start | bytes 3145728 | tf_op jit(solution)/shard_map/psum | solution.py:203
  37.1 22.6 %copy-start.55 = (f32[768]{0:T(1024)S(1)}, f32[768]{0:T(1024)}, u32[]{:S(2)}) copy-start(f32[768]{0:T(1024)} %param.35) | copy-start | bytes 9220
  42.2 20.3 %copy-start.49 = (f32[768]{0:T(1024)S(1)}, f32[768]{0:T(1024)}, u32[]{:S(2)}) copy-start(f32[768]{0:T(1024)} %param.36) | copy-start | bytes 9220
  42.2 20.3 %copy-start.59 = (f32[1536]{0:T(1024)S(1)}, f32[1536]{0:T(1024)}, u32[]{:S(2)}) copy-start(f32[1536]{0:T(1024)} %param.39) | copy-start | bytes 18436
  42.2 20.3 %copy-start.60 = (f32[768]{0:T(1024)S(1)}, f32[768]{0:T(1024)}, u32[]{:S(2)}) copy-start(f32[768]{0:T(1024)} %param.37) | copy-start | bytes 9220
  61.4 10.5 %copy-start.1 = (f32[512,768]{1,0:T(8,128)}, f32[512,768]{1,0:T(8,128)S(1)}, u32[]{:S(2)}) copy-start(f32[512,768]{1,0:T(8,128)S(1)} %get-tuple-element.123) | copy-start | bytes 4718596
  61.4 10.5 %copy-start.39 = (f32[512]{0:T(512)}, f32[512]{0:T(512)S(1)}, u32[]{:S(2)}) copy-start(f32[512]{0:T(512)S(1)} %broadcast_multiply_fusion.2) | copy-start | bytes 6148
  62.5 9.4 copy-start.47
  62.5 10.6 %copy-start.56 = (bf16[1536,768]{1,0:T(8,128)(2,1)S(1)}, bf16[1536,768]{1,0:T(8,128)(2,1)}, u32[]{:S(2)}) copy-start(bf16[1536,768]{1,0:T(8,128)(2,1)} %param.40) | copy-start | bytes 7077892
  75.8 460.0 %all-reduce.13.cloned.1.call-start = ((), (), s32[]{:S(2)}) async-start(), calls=%async_computation.2 | async-start | bytes 3145728 | tf_op jit(solution)/shard_map/psum | solution.py:268
  75.9 253.7 %copy-start.36 = (pred[32,16]{1,0:T(8,128)(4,1)S(1)}, pred[32,16]{1,0:T(8,128)(4,1)}, u32[]{:S(2)}) copy-start(pred[32,16]{1,0:T(8,128)(4,1)} %copy-done.35) | copy-start | bytes 1540
  75.9 254.0 %copy-start.65 = (u32[32]{0:T(128)S(1)}, u32[32]{0:T(128)}, u32[]{:S(2)}) copy-start(u32[32]{0:T(128)} %constant.201) | copy-start | bytes 388
  75.9 257.1 %copy-start.51 = (s32[512]{0:T(512)S(1)}, s32[512]{0:T(512)}, u32[]{:S(2)}) copy-start(s32[512]{0:T(512)} %param.26) | copy-start | bytes 6148
  328.8 92.6 %copy-start.53 = (f32[768]{0:T(1024)S(1)}, f32[768]{0:T(1024)}, u32[]{:S(2)}) copy-start(f32[768]{0:T(1024)} %param.41) | copy-start | bytes 9220
  421.4 46.0 %copy-start.52 = (s32[32]{0:T(128)S(1)}, s32[32]{0:T(128)}, u32[]{:S(2)}) copy-start(s32[32]{0:T(128)} %param.29) | copy-start | bytes 388
  421.4 45.5 %copy-start.12 = (bf16[512,768]{1,0:T(8,128)(2,1)S(1)}, bf16[512,768]{1,0:T(8,128)(2,1)}, u32[]{:S(2)}) copy-start(bf16[512,768]{1,0:T(8,128)(2,1)} %all_gather.16) | copy-start | bytes 2359300
  517.5 70.2 %all-reduce.15.cloned.1.call-start = ((), (), s32[]{:S(2)}) async-start(), calls=%async_computation.3 | async-start | bytes 3145728 | tf_op jit(solution)/shard_map/psum | solution.py:327
  523.2 15.2 %copy-start.46 = (f32[512]{0:T(512)S(1)}, f32[512]{0:T(512)}, u32[]{:S(2)}) copy-start(f32[512]{0:T(512)} %copy-done.45) | copy-start | bytes 6148
  565.9 428.8 %all-reduce.17.cloned.1.call-start = ((), (), s32[]{:S(2)}) async-start(), calls=%async_computation.4 | async-start | bytes 28311552 | tf_op jit(solution)/shard_map/psum | solution.py:330
  578.1 11.6 %copy-start.44 = (f32[512]{0:T(512)S(1)}, f32[512]{0:T(512)}, u32[]{:S(2)}) copy-start(f32[512]{0:T(512)} %copy-done.43) | copy-start | bytes 6148
  (69 other events, 226.1 us)
Sparse Core Ops, SparseCore 0:
  36.6 23.0 all-reduce.8
  75.9 21.5 all-reduce.10
  517.6 18.1 all-reduce.12
  566.0 21.5 all-reduce.14
  595.0 399.6 all-reduce.16
where the time goes:
time: 1020 us; the launch traced here: 1010 us
  waiting for transfers between devices  355 us (35%)
  matrix products  253 us (25%)
  blocking collectives  253 us (25%)
  local copies, waits for them, and re-layouts  64.2 us (6%)
  other arithmetic  38.8 us (4%)
  loops' own time  29 us (3%)
  between operations  19.9 us (2%)
    psum x1, waiting for transfers between devices, local(): lax.psum((grad_qkv, grad_b_qv, grad_w_out, grad_b_out, grad_w_up, grad_b_...  317 us
    psum x1, blocking collectives, local(): lax.psum((grad_qkv, grad_b_qv, grad_w_out, grad_b_out, grad_w_up, grad_b_...  83 us
    dot_general x4, matrix products, image_block(): jnp.einsum('bsf,fd->bsd', hidden, locked_narrowing_matrix, preferred_elem...  77.5 us
    all_gather x1, blocking collectives, local(): lax.all_gather(picture_feature_matrix.astype(jnp.float32), 'dp', axis=0,...  45.8 us
    all_gather x1, blocking collectives, local(): text_piece = lax.all_gather(text_emb, 'dp', axis=0, tiled=True)  42.8 us
    all_gather x1, blocking collectives, local(): lax.all_gather(picture_feature_matrix, 'dp', axis=0, tiled=True)  42.6 us
    unnamed x1, blocking collectives  36.5 us
    dot_general x12, matrix products, project(): jnp.einsum('bsd,de->bse', normed, weight, preferred_element_type=jnp.floa...  31.8 us
  transfers between devices with their start and end apart: 5, of which 4 were waited for; matrix products, arithmetic and copies ran while one was open for 25% of the time, Pallas kernels for 0%

commit v1 on v0

v1 whole, which is shorter than its diff:
```python
import jax
import jax.numpy as jnp
from jax import lax
from jax.sharding import PartitionSpec as P

HEAD = 64
IMG_TOK = 145
LOW_TOK = 50


EPS_TEXT = 1e-05
EPS_UNIT = 1e-06
MASKED_SCORE = -1e30
BF16 = jnp.bfloat16
F32 = jnp.float32


def layer_norm(values, gain, shift, epsilon):
    centered = values - jnp.mean(values, axis=-1, keepdims=True)
    variance = jnp.mean(centered * centered, axis=-1, keepdims=True)
    return centered * lax.rsqrt(variance + epsilon) * gain + shift


def text_norm(values, gain, shift):
    return layer_norm(values, gain, shift, EPS_TEXT)


def gelu_exact(values):
    return jax.nn.gelu(values, approximate=False)


def mp_other(values):
    return lax.ppermute(values, "mp", [(0, 1), (1, 0)])


def mp_sum(values):
    return values + mp_other(values)


def dp_gather(values):
    size = lax.axis_size("dp")
    copies = jnp.broadcast_to(values[None], (size,) + values.shape)
    return lax.all_to_all(copies, "dp", 0, 0, tiled=True)


def mp_join(values):
    other = mp_other(values)
    first = lax.axis_index("mp") == 0
    return jnp.concatenate(
        [jnp.where(first, values, other), jnp.where(first, other, values)], axis=1
    )


def image_block(
    tokens,
    live_len,
    locked_layernorm_gammas,
    locked_mixer_triple_matrix,
    locked_mixer_result_matrix,
    locked_widening_matrix,
    locked_narrowing_matrix,
):
    batch_size, seq_len, model_width = tokens.shape
    heads_all = model_width // HEAD
    tokens_f = tokens.astype(jnp.float32)
    normed = layer_norm(tokens_f, locked_layernorm_gammas[0], 0.0, EPS_UNIT).astype(jnp.bfloat16)

    def project(weight):
        return (
            jnp.einsum("bsd,de->bse", normed, weight, preferred_element_type=jnp.float32)
            .astype(jnp.bfloat16)
            .reshape(batch_size, seq_len, heads_all, HEAD)
        )

    queries, keys_in, values = (
        project(locked_mixer_triple_matrix[0]),
        project(locked_mixer_triple_matrix[1]),
        project(locked_mixer_triple_matrix[2]),
    )
    scores = jnp.einsum(
        "bqhe,bkhe->bhqk", queries, keys_in, preferred_element_type=jnp.float32
    ) * HEAD ** (-0.5)
    key_live = jnp.arange(seq_len, dtype=jnp.int32)[None, :] < live_len[:, None]
    scores = jnp.where(key_live[:, None, None, :], scores, MASKED_SCORE)
    soft_weights = jax.nn.softmax(scores, axis=-1).astype(jnp.bfloat16)
    mixed_heads = (
        jnp.einsum("bhqk,bkhe->bqhe", soft_weights, values, preferred_element_type=jnp.float32)
        .astype(jnp.bfloat16)
        .reshape(batch_size, seq_len, model_width)
    )
    residual = tokens_f + jnp.einsum(
        "bsc,cd->bsd", mixed_heads, locked_mixer_result_matrix, preferred_element_type=jnp.float32
    )
    normed2 = layer_norm(residual, locked_layernorm_gammas[1], 0.0, EPS_UNIT).astype(jnp.bfloat16)
    hidden = gelu_exact(
        jnp.einsum(
            "bsd,df->bsf", normed2, locked_widening_matrix, preferred_element_type=jnp.float32
        )
    ).astype(jnp.bfloat16)
    live = key_live.astype(jnp.float32)[:, :, None]
    return jnp.sum(residual * live, axis=1), jnp.sum(hidden.astype(F32) * live, axis=1)


def wide_dot(left, right):
    high = left.astype(BF16)
    rest = (left - high.astype(F32)).astype(BF16)
    return jnp.dot(high, right, preferred_element_type=F32) + jnp.dot(
        rest, right, preferred_element_type=F32
    )


def local(
    sentence_layer_entry,
    sentence_word_ids,
    picture_tile_activations,
    picture_detail_flag,
    matched_picture_ids,
    mixer_layernorm_gamma,
    mixer_layernorm_offset,
    mixer_triple_matrix,
    mixer_pair_offsets,
    mixer_result_matrix,
    mixer_result_offset,
    perceptron_layernorm_gamma,
    perceptron_layernorm_offset,
    widening_matrix,
    widening_offset,
    narrowing_matrix,
    narrowing_offset,
    sharpening_log,
    locked_layernorm_gammas,
    locked_mixer_triple_matrix,
    locked_mixer_result_matrix,
    locked_widening_matrix,
    locked_narrowing_matrix,
):
    captions = matched_picture_ids.shape[0]
    tokens = sentence_layer_entry.shape[0]
    cap_len = tokens // captions
    model_width = sentence_layer_entry.shape[1]
    local_heads = mixer_triple_matrix.shape[2] // HEAD
    local_width = local_heads * HEAD
    head_scale = HEAD ** (-0.5)
    devices = lax.axis_size("dp")
    all_pairs = captions * devices
    core = lax.axis_index("mp")
    valid = (sentence_word_ids != 0).reshape(captions, cap_len)
    valid_f = valid.astype(jnp.float32)
    count = jnp.sum(valid_f, axis=1, keepdims=True)
    local_images = picture_tile_activations.shape[0]
    img_block = 4
    image_live = jnp.where(picture_detail_flag == 1, IMG_TOK, LOW_TOK).astype(jnp.int32)

    def to_heads(values):
        return values.reshape(captions, cap_len, local_heads, HEAD)

    x_float = sentence_layer_entry.astype(jnp.float32)
    normed_f, norm1_pull = jax.vjp(
        text_norm, x_float, mixer_layernorm_gamma, mixer_layernorm_offset
    )
    normed = normed_f.astype(jnp.bfloat16)
    queries = to_heads(
        (
            jnp.dot(normed, mixer_triple_matrix[0], preferred_element_type=jnp.float32)
            + mixer_pair_offsets[0]
        ).astype(jnp.bfloat16)
    )
    keys_low = to_heads(
        jnp.dot(normed, mixer_triple_matrix[1], preferred_element_type=jnp.float32).astype(
            jnp.bfloat16
        )
    )
    values_low = to_heads(
        (
            jnp.dot(normed, mixer_triple_matrix[2], preferred_element_type=jnp.float32)
            + mixer_pair_offsets[1]
        ).astype(jnp.bfloat16)
    )
    scores = (
        jnp.einsum("gqhe,gkhe->ghqk", queries, keys_low, preferred_element_type=jnp.float32)
        * head_scale
    )
    scores = jnp.where(valid[:, None, None, :], scores, MASKED_SCORE)
    soft_f = jax.nn.softmax(scores, axis=-1)
    soft_low = soft_f.astype(jnp.bfloat16)
    mixed_heads = jnp.einsum(
        "ghqk,gkhe->gqhe", soft_low, values_low, preferred_element_type=jnp.float32
    ).astype(jnp.bfloat16)
    mixed_rows = mixed_heads.reshape(tokens, local_width)
    attended = mp_sum(
        jnp.dot(mixed_rows, mixer_result_matrix, preferred_element_type=jnp.float32)
    )

    def image_group(pieces):
        return image_block(
            pieces[0],
            pieces[1],
            locked_layernorm_gammas,
            locked_mixer_triple_matrix,
            locked_mixer_result_matrix,
            locked_widening_matrix,
            locked_narrowing_matrix,
        )

    resid_sum, hidden_sum = lax.map(
        image_group,
        (
            picture_tile_activations.reshape(
                local_images // img_block, img_block, picture_tile_activations.shape[1], model_width
            ),
            image_live.reshape(local_images // img_block, img_block),
        ),
    )
    resid_sum = resid_sum.reshape(local_images, model_width)
    hidden_sum = hidden_sum.reshape(local_images, -1)
    image_pooled = (
        resid_sum + wide_dot(hidden_sum, locked_narrowing_matrix)
    ) / image_live.astype(F32)[:, None]
    image_emb = (
        image_pooled
        * lax.rsqrt(jnp.sum(image_pooled * image_pooled, axis=-1, keepdims=True) + EPS_UNIT)
    ).astype(BF16)
    all_images = mp_join(dp_gather(image_emb)).reshape(all_pairs, model_width)

    residual = x_float + attended + mixer_result_offset
    normed2_f, norm2_pull = jax.vjp(
        text_norm, residual, perceptron_layernorm_gamma, perceptron_layernorm_offset
    )
    normed2 = normed2_f.astype(jnp.bfloat16)
    pre_act = (
        jnp.dot(normed2, widening_matrix, preferred_element_type=jnp.float32) + widening_offset
    )
    hidden_f, gelu_pull = jax.vjp(gelu_exact, pre_act)
    hidden = hidden_f.astype(jnp.bfloat16)

    def caption_sum(rows):
        return jnp.sum(
            rows.astype(F32).reshape(captions, cap_len, rows.shape[1]) * valid_f[:, :, None], axis=1
        )

    hidden_sums = caption_sum(hidden)
    branch_two = mp_sum(wide_dot(hidden_sums, narrowing_matrix))
    pooled = (caption_sum(residual) + branch_two) / count + narrowing_offset
    inverse = lax.rsqrt(jnp.sum(pooled * pooled, axis=-1, keepdims=True) + EPS_UNIT)
    text_unit = pooled * inverse
    text_emb = text_unit.astype(jnp.bfloat16)
    all_hidden_sums = dp_gather(hidden_sums.astype(BF16)).reshape(all_pairs, -1)

    scale = jnp.exp(sharpening_log[0])
    logits = scale * jnp.einsum(
        "cd,nd->cn", text_emb, all_images, preferred_element_type=jnp.float32
    )
    powers = jnp.exp(logits)
    row_sum = jnp.sum(powers, axis=1, keepdims=True)
    col_sum = jnp.sum(dp_gather(jnp.sum(powers, axis=0)), axis=0)
    is_positive = (
        matched_picture_ids[:, None] == jnp.arange(all_pairs, dtype=jnp.int32)[None, :]
    ).astype(F32)
    positive = jnp.sum(is_positive * logits)
    row_part = jnp.sum(jnp.log(row_sum)) - 2.0 * positive
    col_part = jnp.sum(jnp.log(col_sum))
    score_derivative = (
        powers / row_sum + powers / col_sum[None, :] - 2.0 * is_positive
    ) / (2.0 * all_pairs)
    temp_grad = jnp.sum(score_derivative * logits)
    text_grad = jnp.dot(
        (score_derivative * scale).astype(BF16), all_images, preferred_element_type=jnp.float32
    )
    grad_caption = (
        text_grad - text_unit * jnp.sum(text_unit * text_grad, axis=-1, keepdims=True)
    ) * (inverse / count)
    grad_caption_low = grad_caption.astype(BF16)

    half = captions // 2
    mine = lax.dynamic_slice_in_dim(grad_caption_low, core * half, half, 0)
    all_caption_grads = mp_join(dp_gather(mine)).reshape(all_pairs, model_width)
    grad_w_down = jnp.einsum(
        "cf,cd->fd", all_hidden_sums, all_caption_grads, preferred_element_type=jnp.float32
    )
    grad_b_down = jnp.sum(grad_caption_low.astype(F32) * count, axis=0)

    def spread(rows):
        return (rows[:, None, :] * valid_f[:, :, None]).reshape(tokens, rows.shape[1])

    (grad_pre,) = gelu_pull(
        spread(
            jnp.einsum(
                "td,fd->tf", grad_caption_low, narrowing_matrix, preferred_element_type=jnp.float32
            )
        )
    )
    grad_pre_low = grad_pre.astype(jnp.bfloat16)
    grad_b_up = jnp.sum(grad_pre_low.astype(jnp.float32), axis=0)
    grad_w_up = jnp.einsum("td,tf->df", normed2, grad_pre_low, preferred_element_type=jnp.float32)
    grad_normed2 = mp_sum(
        jnp.einsum("tf,df->td", grad_pre_low, widening_matrix, preferred_element_type=jnp.float32)
    )
    grad_res_norm, grad_ln2_gain, grad_ln2_bias = norm2_pull(grad_normed2)
    grad_residual = spread(grad_caption) + grad_res_norm
    grad_branch1 = grad_residual.astype(jnp.bfloat16)
    grad_b_out = jnp.sum(grad_branch1.astype(jnp.float32), axis=0)
    grad_w_out = jnp.einsum(
        "tc,td->cd", mixed_rows, grad_branch1, preferred_element_type=jnp.float32
    )
    grad_mixed = to_heads(
        jnp.einsum(
            "td,cd->tc", grad_branch1, mixer_result_matrix, preferred_element_type=jnp.float32
        ).astype(jnp.bfloat16)
    )
    grad_soft = jnp.einsum(
        "gqhe,gkhe->ghqk", grad_mixed, values_low, preferred_element_type=jnp.float32
    )
    grad_values = jnp.einsum(
        "ghqk,gqhe->gkhe", soft_low, grad_mixed, preferred_element_type=jnp.float32
    ).astype(jnp.bfloat16)
    grad_scores = (
        soft_f * (grad_soft - jnp.sum(grad_soft * soft_f, axis=-1, keepdims=True))
    ).astype(jnp.bfloat16)
    grad_queries = (
        jnp.einsum("ghqk,gkhe->gqhe", grad_scores, keys_low, preferred_element_type=jnp.float32)
        * head_scale
    ).astype(jnp.bfloat16)
    grad_keys = (
        jnp.einsum("ghqk,gqhe->gkhe", grad_scores, queries, preferred_element_type=jnp.float32)
        * head_scale
    ).astype(jnp.bfloat16)
    flat_grads = (
        grad_queries.reshape(tokens, local_width),
        grad_keys.reshape(tokens, local_width),
        grad_values.reshape(tokens, local_width),
    )
    grad_qkv = jnp.stack(
        [
            jnp.einsum("td,tc->dc", normed, part_grad, preferred_element_type=jnp.float32)
            for part_grad in flat_grads
        ]
    )
    grad_b_qv = jnp.stack(
        [
            jnp.sum(flat_grads[0].astype(jnp.float32), axis=0),
            jnp.sum(flat_grads[2].astype(jnp.float32), axis=0),
        ]
    )
    normed_terms = sum(
        jnp.einsum(
            "tc,dc->td", flat_grads[part], mixer_triple_matrix[part], preferred_element_type=F32
        )
        for part in range(3)
    )
    grad_normed = mp_sum(normed_terms)
    grad_in_norm, grad_ln1_gain, grad_ln1_bias = norm1_pull(grad_normed)
    grad_input = grad_residual + grad_in_norm

    big = lax.psum((grad_qkv.astype(BF16), grad_w_out.astype(BF16), grad_w_up.astype(BF16)), "dp")
    small = (
        grad_b_qv,
        grad_b_out,
        grad_b_up,
        grad_b_down,
        grad_ln1_gain,
        grad_ln1_bias,
        grad_ln2_gain,
        grad_ln2_bias,
        temp_grad.reshape(1),
        row_part.reshape(1),
    )
    packed = jnp.concatenate([part.reshape(-1) for part in small])
    padding = -packed.shape[0] % 1024
    packed = jnp.pad(packed, (0, padding)).reshape(-1, 128)
    packed = jnp.sum(dp_gather(packed), axis=0).reshape(-1)
    sums, start = [], 0
    for part in small:
        sums.append(packed[start : start + part.size].reshape(part.shape))
        start += part.size
    training_error = (sums[9] + col_part) / (2.0 * all_pairs)
    return (
        training_error,
        grad_input,
        big[0].astype(F32),
        sums[0],
        big[1].astype(F32),
        sums[1],
        big[2].astype(F32),
        sums[2],
        grad_w_down,
        sums[3],
        sums[4],
        sums[5],
        sums[6],
        sums[7],
        sums[8],
    )


def solution(mesh):
    placed = (
        P("dp", None),
        P("dp"),
        P(("dp", "mp"), None, None),
        P(("dp", "mp")),
        P("dp"),
        P(),
        P(),
        P(None, None, "mp"),
        P(None, "mp"),
        P("mp", None),
        P(),
        P(),
        P(),
        P(None, "mp"),
        P("mp"),
        P("mp", None),
        P(),
        P(),
        P(),
        P(),
        P(),
        P(),
        P(),
    )
    return jax.shard_map(
        local,
        mesh=mesh,
        in_specs=placed,
        out_specs=(
            P(),
            P("dp", None),
            P(None, None, "mp"),
            P(None, "mp"),
            P("mp", None),
            P(),
            P(None, "mp"),
            P("mp"),
            P("mp", None),
            P(),
            P(),
            P(),
            P(),
            P(),
            P(),
        ),
        check_vma=False,
    )
```

time: 1020 us -> 619 us (0.61)
  blocking collectives: 253 us -> 21 us
  waiting for transfers between devices: 355 us -> 162 us
  starting transfers between devices: 0.95 us -> 33.9 us
  loops' own time: 29 us -> 1.16 us
  other arithmetic: 38.8 us -> 63.4 us
  matrix products: 253 us -> 242 us
    psum x5 -> x1, waiting for transfers between devices: 354 us -> 107 us  [local(): lax.psum((grad_qkv.astype(BF16), grad_w_out.astype(BF16), grad_w_up.astyp...]
    all_gather x4 -> x0, blocking collectives: 133 us -> none  [the longest x1 45.8 us: local(): lax.all_gather(picture_feature_matrix.astype(jnp.float32), 'dp', axis=0,...]
    psum x1 -> x0, blocking collectives: 83 us -> none  [local(): lax.psum((grad_qkv, grad_b_qv, grad_w_out, grad_b_out, grad_w_up, grad_b_...]
    dot_general x14 -> x11, matrix products: 97.4 us -> 23 us  [the longest x3 7.55 us: local(): jnp.einsum('tc,dc->td', flat_grads[part], mixer_triple_matrix[part], pref...]
    dot_general x4, matrix products: 20.4 us -> 79.5 us  [image_block(): jnp.einsum('bsd,df->bsf', normed2, locked_widening_matrix, preferred_elem...]
    all_to_all x0 -> x4, waiting for transfers between devices: none -> 53.1 us  [dp_gather(): return lax.all_to_all(copies, 'dp', 0, 0, tiled=True)]
    unnamed x1 -> x0, blocking collectives: 36.5 us -> none
    all_to_all x0 -> x4, starting transfers between devices: none -> 32.4 us  [dp_gather(): return lax.all_to_all(copies, 'dp', 0, 0, tiled=True)]
  transfers between devices with their start and end apart: 5 -> 11, of which waited for: 4 -> 6; matrix products, arithmetic and copies ran while one was open for 25% -> 49% of each run, Pallas kernels for 0% -> 0%
where the time goes in v1:
time: 619 us; the launch traced here: 610 us
  matrix products  242 us (39%)
  waiting for transfers between devices  162 us (26%)
  local copies, waits for them, and re-layouts  68.1 us (11%)
  other arithmetic  63.4 us (10%)
  starting transfers between devices  33.9 us (5%)
  blocking collectives  21 us (3%)
  between operations  19.6 us (3%)
    psum x1, waiting for transfers between devices, local(): lax.psum((grad_qkv.astype(BF16), grad_w_out.astype(BF16), grad_w_up.astyp...  107 us
    dot_general x4, matrix products, image_block(): jnp.einsum('bsd,df->bsf', normed2, locked_widening_matrix, preferred_elem...  79.5 us
    all_to_all x4, waiting for transfers between devices, dp_gather(): return lax.all_to_all(copies, 'dp', 0, 0, tiled=True)  53.1 us
    all_to_all x4, starting transfers between devices, dp_gather(): return lax.all_to_all(copies, 'dp', 0, 0, tiled=True)  32.4 us
    dot_general x12, matrix products, project(): jnp.einsum('bsd,de->bse', normed, weight, preferred_element_type=jnp.floa...  31.9 us
    sub x4, matrix products, image_block(): soft_weights = jax.nn.softmax(scores, axis=-1).astype(jnp.bfloat16)  31.7 us
    all_to_all x1, blocking collectives, dp_gather(): return lax.all_to_all(copies, 'dp', 0, 0, tiled=True)  21 us
    dot_general x4, matrix products, image_block(): jnp.einsum('bhqk,bkhe->bqhe', soft_weights, values, preferred_element_typ...  18.6 us
  transfers between devices with their start and end apart: 11, of which 6 were waited for; matrix products, arithmetic and copies ran while one was open for 49% of the time, Pallas kernels for 0%

profile of v1, /device:TPU:0, one launch (start us, length us, event | category | flops | bytes accessed | tf_op | source)
XLA Modules:
  0.0 610.4 jit_solution(13249973350091480600)
XLA Ops:
  35.1 5.1 copy.104
  40.2 208.4 %while.12 = (s32[]{:T(128)}, f32[4,4,768]{2,1,0:T(4,128)}, f32[4,4,3072]{2,1,0:T(4,128)S(1)}, bf16[4,4,145,768]{3,2,1,0:T(8,128)(2,1)}, f32[2,768]{1,0:T(2,128)S...) while((s32[]{:T(128)}, f32[4,4,768]{2,1,0:T(4,128)}, ...), condition=%wide.region_19.20_spmd, body=%wide.region_10.19_spmd.sunk | while | flops 5875605504 | bytes 60001060 | solution.py:205
  56.4 7.9 %fusion.225 = (f32[4,12,145]{2,1,0:T(8,128)S(1)}, f32[4,12,145,145]{2,3,1,0:T(8,128)}) fusion(bf16[4,145,12,64]{1,3,2,0:T(8,128)(2,1)} %bitcast.221, bf16[4,145,12,64]{1,3,2,0:T(8,128)(2,1)} %bitcast.220, pred[4,145]{1,0:T(4,128)(4,1)S(1)} %get-tuple-element.225), kind=kOutput, calls=%fused_computation.264.clone.1 | convolution fusion | flops 133214544 | bytes 5846980 | tf_op jit(solution)/shard_map/while/body/eval_jaxpr/sub | solution.py:85
  64.3 4.6 fusion.226
  72.1 19.9 %multiply_reduce_fusion.16 = f32[4,3072]{1,0:T(4,128)S(1)} fusion(f32[4,145]{1,0:T(4,128)S(1)} %get-tuple-element.230, bf16[768,3072]{1,0:T(8,128)(2,1)S(1)} %bitcast.227, f32[4,145,768]{2,1,0:T(8,128)S(1)} %get-tuple-element.228, f32[768]{0:T(1024)S(1)} %get-tuple-element.232, f32[4,145]{1,0:T(4,128)S(1)} %add_rsqrt_fusion.7, ...), kind=kOutput, calls=%fused_computation.5.clone.1 | convolution fusion | flops 2859712512 | bytes 6559536 | tf_op jit(solution)/shard_map/while/body/eval_jaxpr/bsd,df->bsf/dot_general | solution.py:96
  108.3 7.9 %fusion.225 = (f32[4,12,145]{2,1,0:T(8,128)S(1)}, f32[4,12,145,145]{2,3,1,0:T(8,128)}) fusion(bf16[4,145,12,64]{1,3,2,0:T(8,128)(2,1)} %bitcast.221, bf16[4,145,12,64]{1,3,2,0:T(8,128)(2,1)} %bitcast.220, pred[4,145]{1,0:T(4,128)(4,1)S(1)} %get-tuple-element.225), kind=kOutput, calls=%fused_computation.264.clone.1 | convolution fusion | flops 133214544 | bytes 5846980 | tf_op jit(solution)/shard_map/while/body/eval_jaxpr/sub | solution.py:85
  116.2 4.6 fusion.226
  124.0 19.9 %multiply_reduce_fusion.16 = f32[4,3072]{1,0:T(4,128)S(1)} fusion(f32[4,145]{1,0:T(4,128)S(1)} %get-tuple-element.230, bf16[768,3072]{1,0:T(8,128)(2,1)S(1)} %bitcast.227, f32[4,145,768]{2,1,0:T(8,128)S(1)} %get-tuple-element.228, f32[768]{0:T(1024)S(1)} %get-tuple-element.232, f32[4,145]{1,0:T(4,128)S(1)} %add_rsqrt_fusion.7, ...), kind=kOutput, calls=%fused_computation.5.clone.1 | convolution fusion | flops 2859712512 | bytes 6559536 | tf_op jit(solution)/shard_map/while/body/eval_jaxpr/bsd,df->bsf/dot_general | solution.py:96
  160.3 7.9 %fusion.225 = (f32[4,12,145]{2,1,0:T(8,128)S(1)}, f32[4,12,145,145]{2,3,1,0:T(8,128)}) fusion(bf16[4,145,12,64]{1,3,2,0:T(8,128)(2,1)} %bitcast.221, bf16[4,145,12,64]{1,3,2,0:T(8,128)(2,1)} %bitcast.220, pred[4,145]{1,0:T(4,128)(4,1)S(1)} %get-tuple-element.225), kind=kOutput, calls=%fused_computation.264.clone.1 | convolution fusion | flops 133214544 | bytes 5846980 | tf_op jit(solution)/shard_map/while/body/eval_jaxpr/sub | solution.py:85
  168.2 4.6 fusion.226
  175.9 19.9 %multiply_reduce_fusion.16 = f32[4,3072]{1,0:T(4,128)S(1)} fusion(f32[4,145]{1,0:T(4,128)S(1)} %get-tuple-element.230, bf16[768,3072]{1,0:T(8,128)(2,1)S(1)} %bitcast.227, f32[4,145,768]{2,1,0:T(8,128)S(1)} %get-tuple-element.228, f32[768]{0:T(1024)S(1)} %get-tuple-element.232, f32[4,145]{1,0:T(4,128)S(1)} %add_rsqrt_fusion.7, ...), kind=kOutput, calls=%fused_computation.5.clone.1 | convolution fusion | flops 2859712512 | bytes 6559536 | tf_op jit(solution)/shard_map/while/body/eval_jaxpr/bsd,df->bsf/dot_general | solution.py:96
  212.2 7.9 %fusion.225 = (f32[4,12,145]{2,1,0:T(8,128)S(1)}, f32[4,12,145,145]{2,3,1,0:T(8,128)}) fusion(bf16[4,145,12,64]{1,3,2,0:T(8,128)(2,1)} %bitcast.221, bf16[4,145,12,64]{1,3,2,0:T(8,128)(2,1)} %bitcast.220, pred[4,145]{1,0:T(4,128)(4,1)S(1)} %get-tuple-element.225), kind=kOutput, calls=%fused_computation.264.clone.1 | convolution fusion | flops 133214544 | bytes 5846980 | tf_op jit(solution)/shard_map/while/body/eval_jaxpr/sub | solution.py:85
  220.1 4.6 fusion.226
  227.9 19.9 %multiply_reduce_fusion.16 = f32[4,3072]{1,0:T(4,128)S(1)} fusion(f32[4,145]{1,0:T(4,128)S(1)} %get-tuple-element.230, bf16[768,3072]{1,0:T(8,128)(2,1)S(1)} %bitcast.227, f32[4,145,768]{2,1,0:T(8,128)S(1)} %get-tuple-element.228, f32[768]{0:T(1024)S(1)} %get-tuple-element.232, f32[4,145]{1,0:T(4,128)S(1)} %add_rsqrt_fusion.7, ...), kind=kOutput, calls=%fused_computation.5.clone.1 | convolution fusion | flops 2859712512 | bytes 6559536 | tf_op jit(solution)/shard_map/while/body/eval_jaxpr/bsd,df->bsf/dot_general | solution.py:96
  254.2 21.0 %all_to_all.26 = bf16[16,16,768]{2,1,0:T(8,128)(2,1)S(1)} all-to-all(bf16[16,16,768]{2,1,0:T(8,128)(2,1)S(1)} %broadcast_in_dim.83), channel_id=1, replica_groups=mesh['dp'=16,'mp'=2] {'dp'}, dimensions={0} | all-to-all | bytes 786432 | tf_op jit(solution)/shard_map/all_to_all | solution.py:43
  286.9 10.0 %fusion.53 = (f32[32,1536]{1,0:T(8,128)S(1)}, f32[512,1536]{1,0:T(8,128)}, f32[512,1536]{1,0:T(8,128)}) fusion(f32[32,16]{1,0:T(8,128)S(1)} %convert_element_type.204, f32[1536]{0:T(1024)S(1)} %copy-done.67, bf16[768,1536]{1,0:T(8,128)(2,1)S(1)} %copy-done, f32[512,768]{1,0:T(8,128)S(1)} %copy-done.1, f32[768]{0:T(1024)S(1)} %copy-done.71, ...), kind=kOutput, calls=%fused_computation.84 | convolution fusion | flops 1264140288 | bytes 10438656 | tf_op jit(solution)/shard_map/dot_general | solution.py:231
  305.5 7.4 %all-to-all-done.1 = f32[16,1,512]{2,1,0:T(1,128)S(1)} async-done(((f32[16,1,512]{2,1,0:T(1,128)}), f32[16,1,512]{2,1,0:T(1,128)S(1)}, u32[]{:S(2)}, u32[]{:S(2)}) %all-to-all-start.1) | async-done | bytes 32800 | tf_op jit(solution)/shard_map/all_to_all | solution.py:43
  330.8 5.0 convolution_convert_fusion.3
  380.1 6.9 %all-to-all-start.3 = ((bf16[16,32,1536]{2,1,0:T(8,128)(2,1)}), bf16[16,32,1536]{2,1,0:T(8,128)(2,1)}, u32[]{:S(2)}, u32[]{:S(2)}) async-start(bf16[16,32,1536]{2,1,0:T(8,128)(2,1)} %broadcast_in_dim.91), calls=%async_computation.3 | async-start | bytes 3145728 | tf_op jit(solution)/shard_map/all_to_all | solution.py:43
  410.4 33.4 %all-to-all-done.3 = bf16[16,32,1536]{2,1,0:T(8,128)(2,1)} async-done(((bf16[16,32,1536]{2,1,0:T(8,128)(2,1)}), bf16[16,32,1536]{2,1,0:T(8,128)(2,1)}, u32[]{:S(2)}, u32[]{:S(2)}) %all-to-all-start.3) | async-done | bytes 1572896 | tf_op jit(solution)/shard_map/all_to_all | solution.py:43
  445.3 17.6 %all-to-all-start.2 = ((f32[16,56,128]{2,1,0:T(8,128)}), f32[16,56,128]{2,1,0:T(8,128)}, u32[]{:S(2)}, u32[]{:S(2)}) async-start(f32[16,56,128]{2,1,0:T(8,128)} %broadcast_in_dim.88), calls=%async_computation.2 | async-start | bytes 917504 | tf_op jit(solution)/shard_map/all_to_all | solution.py:43
  462.9 5.2 convolution_bitcast_fusion
  470.0 12.3 %all-to-all-done.2 = f32[16,56,128]{2,1,0:T(8,128)} async-done(((f32[16,56,128]{2,1,0:T(8,128)}), f32[16,56,128]{2,1,0:T(8,128)}, u32[]{:S(2)}, u32[]{:S(2)}) %all-to-all-start.2) | async-done | bytes 458784 | tf_op jit(solution)/shard_map/all_to_all | solution.py:43
  487.0 107.2 %all-reduce.4.cloned.1.call-done = (bf16[3,768,384]{2,1,0:T(8,128)(2,1)}, bf16[384,768]{1,0:T(8,128)(2,1)}, bf16[768,1536]{1,0:T(8,128)(2,1)}) async-done(((bf16[3,768,384]{2,1,0:T(8,128)(2,1)}, bf16[384,768]{1,0:T(8,128)(2,1)}, bf16[768,1536]{1,0:T(8,128)(2,1)}), (bf16[3,768,384]{2,1,0:T(8,128)(2,1)}, bf16[384,768]{1,0:T(8,128)(2,1)}, bf16[768,1536]{1,0:T(8,128)(2,1)})) %all-reduce.4.cloned.1.call-update) | async-done | bytes 4718608 | tf_op jit(solution)/shard_map/psum | solution.py:354
  (380 shorter events, 228.9 us)
Async XLA Ops:
  7.2 279.7 %copy-start = (bf16[768,1536]{1,0:T(8,128)(2,1)S(1)}, bf16[768,1536]{1,0:T(8,128)(2,1)}, u32[]{:S(2)}) copy-start(bf16[768,1536]{1,0:T(8,128)(2,1)} %param.38) | copy-start | bytes 7077892
  11.6 12.4 %copy-start.50 = (pred[32,16]{1,0:T(8,128)(4,1)}, pred[32,16]{1,0:T(8,128)(4,1)S(1)}, u32[]{:S(2)}) copy-start(pred[32,16]{1,0:T(8,128)(4,1)S(1)} %broadcast_in_dim.76) | copy-start | bytes 1540
  34.1 245.1 %collective-permute-start = (f32[512,768]{1,0:T(8,128)}, f32[512,768]{1,0:T(8,128)}, u32[]{:S(2)}, u32[]{:S(2)}) collective-permute-start(f32[512,768]{1,0:T(8,128)} %fusion.152), channel_id=1, source_target_pairs={{0,1},{1,0},{2,3},{3,2},{4,5},{5,4},{6,7},{7,6},{8,9},{9,8},{10,11... | collective-permute-start | bytes 4718600 | tf_op jit(solution)/shard_map/ppermute | solution.py:33
  253.2 22.0 %copy-start.51 = (pred[32,16]{1,0:T(8,128)(4,1)S(1)}, pred[32,16]{1,0:T(8,128)(4,1)}, u32[]{:S(2)}) copy-start(pred[32,16]{1,0:T(8,128)(4,1)} %copy-done.50) | copy-start | bytes 1540
  254.1 25.1 %copy-start.4 = (bf16[512,768]{1,0:T(8,128)(2,1)S(1)}, bf16[512,768]{1,0:T(8,128)(2,1)}, u32[]{:S(2)}) copy-start(bf16[512,768]{1,0:T(8,128)(2,1)} %param.25) | copy-start | bytes 2359300
  275.2 2.0 collective-permute-start.2
  285.0 11.9 %copy-start.48 = (f32[512]{0:T(512)}, f32[512]{0:T(512)S(1)}, u32[]{:S(2)}) copy-start(f32[512]{0:T(512)S(1)} %broadcast_multiply_fusion.2) | copy-start | bytes 6148
  286.8 10.1 %copy-start.65 = (f32[512]{0:T(512)}, f32[512]{0:T(512)S(1)}, u32[]{:S(2)}) copy-start(f32[512]{0:T(512)S(1)} %multiply_reduce_fusion.6) | copy-start | bytes 6148
  286.9 10.0 %copy-start.56 = (f32[512]{0:T(512)}, f32[512]{0:T(512)S(1)}, u32[]{:S(2)}) copy-start(f32[512]{0:T(512)S(1)} %fusion.130) | copy-start | bytes 6148
  286.9 10.0 %copy-start.5 = (bf16[1536,768]{1,0:T(8,128)(2,1)S(1)}, bf16[1536,768]{1,0:T(8,128)(2,1)}, u32[]{:S(2)}) copy-start(bf16[1536,768]{1,0:T(8,128)(2,1)} %param.40) | copy-start | bytes 7077892
  297.9 1.5 collective-permute-start.1
  301.1 13.5 %copy-start.40 = (f32[32,512]{1,0:T(8,128)}, f32[32,512]{1,0:T(8,128)S(1)}, u32[]{:S(2)}) copy-start(f32[32,512]{1,0:T(8,128)S(1)} %get-tuple-element.150) | copy-start | bytes 196612
  301.8 11.1 %all-to-all-start.1 = ((f32[16,1,512]{2,1,0:T(1,128)}), f32[16,1,512]{2,1,0:T(1,128)S(1)}, u32[]{:S(2)}, u32[]{:S(2)}) async-start(f32[16,1,512]{2,1,0:T(1,128)} %broadcast_in_dim.84), calls=%async_computation.1 | async-start | bytes 65536 | tf_op jit(solution)/shard_map/all_to_all | solution.py:43
  316.0 23.7 %copy-start.27 = (f32[32,768]{1,0:T(8,128)}, f32[32,768]{1,0:T(8,128)S(1)}, u32[]{:S(2)}) copy-start(f32[32,768]{1,0:T(8,128)S(1)} %get-tuple-element.106) | copy-start | bytes 294916
  322.5 8.3 %copy-start.72 = (f32[768]{0:T(1024)S(1)}, f32[768]{0:T(1024)}, u32[]{:S(2)}) copy-start(f32[768]{0:T(1024)} %param.37) | copy-start | bytes 9220
  325.1 10.8 %collective-permute-start.3 = (f32[512,768]{1,0:T(8,128)}, f32[512,768]{1,0:T(8,128)}, u32[]{:S(2)}, u32[]{:S(2)}) collective-permute-start(f32[512,768]{1,0:T(8,128)} %fusion.154), channel_id=1, source_target_pairs={{0,1},{1,0},{2,3},{3,2},{4,5},{5,4},{6,7},{7,6},{8,9},{9,8},{10,11... | collective-permute-start | bytes 4718600 | tf_op jit(solution)/shard_map/ppermute | solution.py:33
  326.5 51.4 %all-to-all-start.4 = ((bf16[16,16,768]{2,1,0:T(8,128)(2,1)}), bf16[16,16,768]{2,1,0:T(8,128)(2,1)}, u32[]{:S(2)}, u32[]{:S(2)}) async-start(bf16[16,16,768]{2,1,0:T(8,128)(2,1)} %broadcast_in_dim.92), calls=%async_computation.4 | async-start | bytes 786432 | tf_op jit(solution)/shard_map/all_to_all | solution.py:43
  330.7 263.5 %all-reduce.4.cloned.1.call-start = ((), (), s32[]{:S(2)}) async-start(), calls=%async_computation.5 | async-start | bytes 9437184 | tf_op jit(solution)/shard_map/psum | solution.py:354
  380.1 63.6 %all-to-all-start.3 = ((bf16[16,32,1536]{2,1,0:T(8,128)(2,1)}), bf16[16,32,1536]{2,1,0:T(8,128)(2,1)}, u32[]{:S(2)}, u32[]{:S(2)}) async-start(bf16[16,32,1536]{2,1,0:T(8,128)(2,1)} %broadcast_in_dim.91), calls=%async_computation.3 | async-start | bytes 3145728 | tf_op jit(solution)/shard_map/all_to_all | solution.py:43
  388.8 13.1 %copy-start.46 = (f32[512]{0:T(512)S(1)}, f32[512]{0:T(512)}, u32[]{:S(2)}) copy-start(f32[512]{0:T(512)} %copy-done.45) | copy-start | bytes 6148
  388.8 13.1 %copy-start.47 = (f32[768]{0:T(1024)S(1)}, f32[768]{0:T(1024)}, u32[]{:S(2)}) copy-start(f32[768]{0:T(1024)} %param.30) | copy-start | bytes 9220
  391.7 10.2 %collective-permute-start.4 = (f32[512,768]{1,0:T(8,128)}, f32[512,768]{1,0:T(8,128)}, u32[]{:S(2)}, u32[]{:S(2)}) collective-permute-start(f32[512,768]{1,0:T(8,128)} %add_add_fusion.3), channel_id=1, source_target_pairs={{0,1},{1,0},{2,3},{3,2},{4,5},{5,4},{6,7},{7,6},{8,9},{9,8},{10,11... | collective-permute-start | bytes 4718600 | tf_op jit(solution)/shard_map/ppermute | solution.py:33
  391.7 4.3 collective-permute-start.5
  445.3 37.1 %all-to-all-start.2 = ((f32[16,56,128]{2,1,0:T(8,128)}), f32[16,56,128]{2,1,0:T(8,128)}, u32[]{:S(2)}, u32[]{:S(2)}) async-start(f32[16,56,128]{2,1,0:T(8,128)} %broadcast_in_dim.88), calls=%async_computation.2 | async-start | bytes 917504 | tf_op jit(solution)/shard_map/all_to_all | solution.py:43
  (76 other events, 261.2 us)
Sparse Core Ops, SparseCore 0:
  375.1 219.1 all-reduce.3
